TPU v7x, 32 devices: a whole 2x2x4 slice. The times are simulated.
32 devices in a mesh: grp: 2 (over x), ctx: 16 (over z, y, core).
Axes of the slice: x: 2, y: 2, z: 4, core: 2. Of those that a mesh axis runs over, the one named last changes fastest.
Arguments:
- hidden: bfloat16 [4, 7168], P('grp', 'ctx'), parts along dimension 0, may hold values from -6 to 6
- q_down: bfloat16 [7168, 1536], P('ctx'), may hold values from -0.0625 to 0.0625
- q_gain: float32 [1536], replicated, may hold values from 0.25 to 1.75
- q_up: bfloat16 [1536, 24576], P(None, 'ctx'), may hold values from -0.15625 to 0.15625
- w_uk: bfloat16 [128, 128, 512], P('ctx'), may hold values from -0.5 to 0.5
- kv_down: bfloat16 [7168, 576], P('ctx'), may hold values from -0.0625 to 0.0625
- kv_gain: float32 [512], replicated, may hold values from 3 to 8
- w_uv: bfloat16 [128, 512, 128], P('ctx'), may hold values from -0.25 to 0.25
- o_proj: bfloat16 [16384, 7168], P('ctx'), may hold values from -0.03125 to 0.03125
- cache: bfloat16 [4, 4096, 576], P('grp', 'ctx'), parts along dimension 0, may hold values from -40 to 40
- lengths: int32 [4], P('grp'), parts along dimension 0, may hold values from 2048 to 4096, as said below
- blocks: int32 [4, 32], P('grp'), parts along dimension 0, may hold values from 0 to 63, as said below
Outputs:
- attn_out: bfloat16 [4, 7168], P('grp', 'ctx'), parts along dimension 0
There are 2 independent parts, one for each index of `grp`. A program takes and returns all parts, laid end to end along the dimension named above; an argument that names none is the same for every part. Nothing has to cross between parts.
Inputs may be any that keep to these rules, and one draw needn't show every extreme that they name: `lengths`: some row fills all 4096 slots. Each row names 32 different blocks, each starting below that row's length; the block of the row's last cached token is always among them.
All inputs are finite; a program needn't handle non-finite values.
Results may differ from a plain program's by a relative error of at most 0.02.
Values may be sent and summed in bfloat16 or wider, within the bound.
A program may use at most 192 MiB of HBM per device.

v0:
```python
import jax
import jax.numpy as jnp
from jax import lax
from jax.sharding import PartitionSpec as P

NOPE = 128
ROPE = 64
BLOCK = 64


def combined_all(value, axis, join):
    pieces = jax.tree.map(lambda part: lax.all_gather(part, axis), value)
    head = jax.tree.map(lambda part: part[0], pieces)
    tail = jax.tree.map(lambda part: part[1:], pieces)
    subtotal, _ = lax.scan(lambda subtotal, section: (join(subtotal, section), None), head, tail)
    return subtotal


def rms_scale(values, gain):
    return values * lax.rsqrt(jnp.mean(values * values, axis=-1, keepdims=True) + 1e-06) * gain


def combine_parts(first, second):
    peak = jnp.maximum(first[0], second[0])
    fac_one = jnp.exp(first[0] - peak)
    fac_two = jnp.exp(second[0] - peak)
    total = first[1] * fac_one + second[1] * fac_two
    numer = first[2] * fac_one[..., None] + second[2] * fac_two[..., None]
    return (peak, total, numer)


def per_device(
    hidden, q_down, q_gain, q_up, w_uk, kv_down, kv_gain, w_uv, o_proj, cache, lengths, blocks
):
    rows = hidden.shape[0]
    local_heads = w_uk.shape[0]
    nope = w_uk.shape[1]
    latent_width = w_uk.shape[2]
    q_part = jnp.dot(hidden, q_down, preferred_element_type=jnp.float32)
    kv_part = jnp.dot(hidden, kv_down, preferred_element_type=jnp.float32)
    q_low, kv_new = lax.psum((q_part, kv_part), "ctx")
    q_normed = rms_scale(q_low, q_gain).astype(jnp.bfloat16)
    q_full = jnp.dot(q_normed, q_up, preferred_element_type=jnp.float32).astype(jnp.bfloat16)
    q_full = q_full.reshape(rows, local_heads, -1)
    q_lat = jnp.einsum(
        "rhn,hnl->rhl", q_full[:, :, :nope], w_uk, preferred_element_type=jnp.float32
    )
    query_local = jnp.concatenate([q_lat, q_full[:, :, nope:].astype(jnp.float32)], axis=-1).astype(
        jnp.bfloat16
    )
    query = lax.all_gather(query_local, "ctx", axis=1, tiled=True)
    lat_new = rms_scale(kv_new[:, :latent_width], kv_gain)
    key_new = jnp.concatenate([lat_new, kv_new[:, latent_width:]], axis=-1).astype(jnp.bfloat16)
    scale = (NOPE + ROPE) ** (-0.5)
    own = scale * jnp.einsum("rhc,rc->rh", query, key_new, preferred_element_type=jnp.float32)
    tok_local = cache.shape[1]
    position = lax.axis_index("ctx") * tok_local + jnp.arange(tok_local, dtype=jnp.int32)
    used = jnp.any((position // BLOCK)[None, None, :] == blocks[:, :, None], axis=1)
    used = used & (position[None, :] < lengths[:, None])
    score = scale * jnp.einsum("rhc,rtc->rht", query, cache, preferred_element_type=jnp.float32)
    peak_local = jnp.max(jnp.where(used[:, None, :], score, -1e30), axis=2)
    expo = jnp.where(used[:, None, :], jnp.exp(score - peak_local[..., None]), 0.0)
    total_local = jnp.sum(expo, axis=2)
    weights = expo.astype(jnp.bfloat16)
    numer_local = jnp.einsum(
        "rht,rtl->rhl", weights, cache[:, :, :latent_width], preferred_element_type=jnp.float32
    )
    head_start = lax.axis_index("ctx") * local_heads
    own_mine = lax.dynamic_slice_in_dim(own, head_start, local_heads, 1)
    peak_all, total_all, numer_all = combined_all(
        (peak_local, total_local, numer_local), "ctx", combine_parts
    )
    peak_mine = lax.dynamic_slice_in_dim(peak_all, head_start, local_heads, 1)
    top = jnp.maximum(peak_mine, own_mine)
    factor = jnp.exp(peak_mine - top)
    total = lax.dynamic_slice_in_dim(total_all, head_start, local_heads, 1) * factor
    numer = lax.dynamic_slice_in_dim(numer_all, head_start, local_heads, 1) * factor[..., None]
    own_weight = jnp.exp(own_mine - top)
    numer = numer + own_weight[..., None] * key_new[:, None, :latent_width].astype(jnp.float32)
    latent = (numer / (total + own_weight)[..., None]).astype(jnp.bfloat16)
    head_out = jnp.einsum("rhl,hlv->rhv", latent, w_uv, preferred_element_type=jnp.float32)
    head_out = head_out.astype(jnp.bfloat16).reshape(rows, -1)
    partial_value = jnp.dot(head_out, o_proj, preferred_element_type=jnp.float32)
    return lax.psum_scatter(partial_value, "ctx", scatter_dimension=1, tiled=True).astype(
        jnp.bfloat16
    )


def solution(mesh):
    placed = (
        P("grp", "ctx"),
        P("ctx", None),
        P(),
        P(None, "ctx"),
        P("ctx", None, None),
        P("ctx", None),
        P(),
        P("ctx", None, None),
        P("ctx", None),
        P("grp", "ctx", None),
        P("grp"),
        P("grp", None),
    )
    return jax.shard_map(
        per_device, mesh=mesh, in_specs=placed, out_specs=P("grp", "ctx"), check_vma=False
    )
```

profile of v0, /device:TPU:0, one launch (start us, length us, event | category | flops | bytes accessed | tf_op | source)
XLA Modules:
  0.0 284.2 jit_solution(18439566627898024171)
XLA Ops:
  6.6 1.4 fusion.27
  9.0 63.0 %all-reduce = (f32[2,1536]{1,0:T(2,128)S(1)}, f32[2,576]{1,0:T(2,128)S(1)}) all-reduce(f32[2,1536]{1,0:T(2,128)S(1)} %fusion.26, f32[2,576]{1,0:T(2,128)S(1)} %fusion.27), channel_id=1, replica_groups=mesh['grp'=2,'ctx'=16] {'ctx'}, use_global_device_ids=true, to_apply=%region_1.0 | all-reduce | flops 4224 | bytes 33792 | tf_op jit(solution)/shard_map/psum | solution.py:41
  72.1 3.1 %convolution_convert_fusion = bf16[2,1536]{1,0:T(2,128)(2,1)S(1)} fusion(bf16[1536,1536]{1,0:T(8,128)(2,1)} %param.17, f32[2,1536]{1,0:T(2,128)S(1)} %get-tuple-element.61, f32[2]{0:T(128)S(1)} %add_rsqrt_fusion.1, f32[1536]{0:T(1024)} %param.16), kind=kOutput, calls=%fused_computation.10 | convolution fusion | flops 9449472 | bytes 4743176 | tf_op jit(solution)/shard_map/dot_general | solution.py:43
  75.4 1.5 fusion.3
  76.9 18.0 %all_gather.21 = bf16[2,128,576]{2,0,1:T(2,128)(2,1)S(1)} all-gather(bf16[2,8,576]{2,0,1:T(2,128)(2,1)S(1)} %pad_maximum_fusion), channel_id=1, replica_groups=mesh['grp'=2,'ctx'=16] {'ctx'}, dimensions={1}, use_global_device_ids=true | all-gather | bytes 313344 | tf_op jit(solution)/shard_map/all_gather | solution.py:51
  97.7 19.4 %all-gather.4 = f32[16,2,128]{2,1,0:T(2,128)S(1)} all-gather(f32[1,2,128]{2,1,0:T(2,128)S(1)} %bitcast.55), channel_id=3, replica_groups=mesh['grp'=2,'ctx'=16] {'ctx'}, dimensions={0}, use_global_device_ids=true | all-gather | bytes 17408 | tf_op jit(solution)/shard_map/all_gather | solution.py:12
  117.1 17.4 %all-gather.3 = f32[16,2,128]{2,1,0:T(2,128)S(1)} all-gather(f32[1,2,128]{2,1,0:T(2,128)S(1)} %bitcast.54), channel_id=2, replica_groups=mesh['grp'=2,'ctx'=16] {'ctx'}, dimensions={0}, use_global_device_ids=true | all-gather | bytes 17408 | tf_op jit(solution)/shard_map/all_gather | solution.py:12
  134.9 36.5 %all-gather.7.cloned.1.call-done = f32[32,128,512]{2,1,0:T(8,128)} async-done(((f32[2,128,512]{2,1,0:T(8,128)}), f32[32,128,512]{2,1,0:T(8,128)}) %all-gather.7.cloned.1.call-update) | async-done | bytes 8388624 | tf_op jit(solution)/shard_map/all_gather | solution.py:12
  171.5 7.9 %slice.66 = f32[30,128,512]{2,1,0:T(8,128)} slice(f32[32,128,512]{2,1,0:T(8,128)} %all-gather.7.cloned.1.call-done), slice={[2:32], [0:128], [0:512]} | slice | bytes 15728640 | tf_op jit(solution)/shard_map/slice | solution.py:14
  179.3 19.0 %while.14 = (s32[]{:T(128)}, f32[2,128]{1,0:T(2,128)S(1)}, f32[2,128]{1,0:T(2,128)S(1)}, f32[2,128,512]{2,1,0:T(8,128)S(1)}, f32[15,2,128]{2,1,0:T(2,128)S(1)}, ...) while((s32[]{:T(128)}, f32[2,128]{1,0:T(2,128)S(1)}, f32[2,128]{1,0:T(2,128)S(1)}, ...), condition=%wide.region_6.7_spmd, body=%wide.region_5.6_spmd.sunk | while | flops 394754 | bytes 1583205 | solution.py:15
  179.4 1.3 fusion.42
  180.7 1.2 fusion.42
  182.0 1.2 fusion.42
  184.5 1.2 fusion.42
  185.7 1.2 fusion.42
  188.3 1.2 fusion.42
  189.5 1.2 fusion.42
  192.0 1.2 fusion.42
  193.3 1.2 fusion.42
  195.8 1.2 fusion.42
  197.1 1.2 fusion.42
  198.5 10.3 %convolution_bitcast_fusion = f32[7168,2]{1,0:T(8,128)} fusion(bf16[1024,7168]{1,0:T(8,128)(2,1)} %param.22, bf16[8,512,128]{2,1,0:T(8,128)(2,1)S(1)} %copy-done.2, bf16[2,8,512]{2,1,0:T(8,128)(2,1)S(1)} %divide_convert_fusion), kind=kOutput, calls=%fused_computation.9 | convolution fusion | flops 31459328 | bytes 15802368
  208.8 66.9 %reduce-scatter.4.cloned.1.call-done = f32[448,2]{1,0:T(8,128)} async-done(((f32[7168,2]{1,0:T(8,128)}), f32[448,2]{1,0:T(8,128)}) %reduce-scatter.4.cloned.1.call-update) | async-done | bytes 3600
  275.7 1.6 copy.32
  (66 shorter events, 9.9 us)
Async XLA Ops:
  6.5 1.5 copy-start
  6.5 89.1 %copy-start.4 = (s32[2,32]{1,0:T(2,128)S(1)}, s32[2,32]{1,0:T(2,128)}, u32[]{:S(2)}) copy-start(s32[2,32]{1,0:T(2,128)} %param.25) | copy-start | bytes 772
  6.5 89.2 %copy-start.5 = (s32[2]{0:T(128)S(1)}, s32[2]{0:T(128)}, u32[]{:S(2)}) copy-start(s32[2]{0:T(128)} %param.24) | copy-start | bytes 28
  6.5 89.3 %copy-start.1 = (bf16[2,256,576]{1,2,0:T(8,128)(2,1)S(1)}, bf16[2,256,576]{1,2,0:T(8,128)(2,1)}, u32[]{:S(2)}) copy-start(bf16[2,256,576]{1,2,0:T(8,128)(2,1)} %param.23) | copy-start | bytes 1769476
  6.5 164.9 %all-gather.7.cloned.1.call-start = ((), (), s32[]{:S(2)}) async-start(), calls=%async_computation.1 | async-start | bytes 8912896 | tf_op jit(solution)/shard_map/all_gather | solution.py:12
  72.1 62.6 %copy-start.3 = (f32[512]{0:T(512)S(1)}, f32[512]{0:T(512)}, u32[]{:S(2)}) copy-start(f32[512]{0:T(512)} %param.20) | copy-start | bytes 6148
  97.4 178.3 %reduce-scatter.4.cloned.1.call-start = ((), (), s32[]{:S(2)}) async-start(), calls=%async_computation.2 | async-start | bytes 3899392
  171.5 7.9 %slice-start = ((f32[32,128,512]{2,1,0:T(8,128)}), f32[2,128,512]{2,1,0:T(8,128)S(1)}, s32[]{:S(2)}) async-start(f32[32,128,512]{2,1,0:T(8,128)} %all-gather.7.cloned.1.call-done), calls=%async_computation.3 | async-start | bytes 1048576 | tf_op jit(solution)/shard_map/slice | solution.py:13
  179.3 19.1 %copy-start.2 = (bf16[8,512,128]{2,1,0:T(8,128)(2,1)S(1)}, bf16[8,512,128]{2,1,0:T(8,128)(2,1)}, u32[]{:S(2)}) copy-start(bf16[8,512,128]{2,1,0:T(8,128)(2,1)} %param.21) | copy-start | bytes 3145732
Sparse Core Ops, SparseCore 0:
  97.5 73.8 all-gather.6
  208.9 66.7 reduce-scatter.3
where the time goes:
time: 285 us; the launch traced here: 284 us
  blocking collectives  118 us (41%)
  waiting for transfers between devices  103 us (36%)
  other arithmetic  19.5 us (7%)
  matrix products  18.9 us (7%)
  between operations  13.5 us (5%)
  local copies, waits for them, and re-layouts  10.4 us (4%)
    unnamed x3, waiting for transfers between devices  67 us
    psum x1, blocking collectives, per_device(): q_low, kv_new = lax.psum((q_part, kv_part), 'ctx')  63 us
    all_gather x2, blocking collectives, combined_all(): pieces = jax.tree.map(lambda part: lax.all_gather(part, axis), value)  36.9 us
    all_gather x1, waiting for transfers between devices, combined_all(): pieces = jax.tree.map(lambda part: lax.all_gather(part, axis), value)  36.5 us
    add x15, other arithmetic, combine_parts(): numer = first[2] * fac_one[..., None] + second[2] * fac_two[..., None]  18.2 us
    all_gather x1, blocking collectives, per_device(): query = lax.all_gather(query_local, 'ctx', axis=1, tiled=True)  18 us
    unnamed x1, matrix products  10.3 us
    slice x3, local copies, waits for them, and re-layouts, combined_all(): tail = jax.tree.map(lambda part: part[1:], pieces)  7.87 us
  transfers between devices with their start and end apart: 2, of which 2 were waited for; matrix products, arithmetic and copies ran while one was open for 0% of the time, Pallas kernels for 0%

commit v1 on v0

v1 whole, which is shorter than its diff:
```python
import functools
import math

import jax
import jax.numpy as jnp
from jax import lax
from jax.experimental import pallas as pl
from jax.experimental.pallas import tpu as pltpu
from jax.sharding import PartitionSpec as P

NOPE = 128
ROPE = 64
BLOCK = 64
LANES = 128
F32 = jnp.float32
BF16 = jnp.bfloat16
MESH = pl.DeviceIdType.MESH


def dot(a, b):
    return jnp.dot(a, b, preferred_element_type=F32)


def split3(value):
    high = value.astype(BF16).astype(F32)
    mid = (value - high).astype(BF16).astype(F32)
    return high, mid, value - high - mid


def kernel(
    n, rows, heads, lat, pad,
    lengths, blocks, hidden, q_gain, kv_gain,
    q_down, kv_down, q_up, w_uk, cache, w_uv, o_proj,
    out,
    v_qd, v_kd, v_qu, v_uk, v_ca, v_uv, v_op,
    s1, r1, g2, qf, qs, qall, s4, r4, s5, r5,
    load_sem, send_sem, recv_sem,
):
    me = lax.axis_index("ctx")
    ql = q_down.shape[1]
    kvw = kv_down.shape[1]
    kr = heads * rows
    head_width = NOPE + ROPE
    q_rows = q_up.shape[0]
    o_rows = o_proj.shape[0]
    scale = head_width ** (-0.5)

    loads = []

    def load(src, dst, parts=1):
        mine = []
        size = src.shape[0] // parts
        for part in range(parts):
            where = pl.ds(part * size, size)
            copy = pltpu.make_async_copy(src.at[where], dst.at[where], load_sem.at[len(loads)])
            copy.start()
            loads.append(copy)
            mine.append(copy)
        return mine

    l_qd = load(q_down, v_qd)
    l_kd = load(kv_down, v_kd)
    l_qu = load(q_up, v_qu, 4)
    l_uk = load(w_uk, v_uk)
    l_ca = load(cache, v_ca)
    l_uv = load(w_uv, v_uv)
    l_op = load(o_proj, v_op, 8)

    def arrive(copies):
        for copy in copies:
            copy.wait()

    barrier = pltpu.get_barrier_semaphore()

    def greet(k, _):
        pl.semaphore_signal(
            barrier, inc=1, device_id={"ctx": lax.rem(me + k, n)}, device_id_type=MESH
        )
        return 0

    lax.fori_loop(1, n, greet, 0)

    def remote(phase, src, dst, peer):
        return pltpu.make_async_remote_copy(
            src_ref=src, dst_ref=dst,
            send_sem=send_sem.at[phase, peer], recv_sem=recv_sem.at[phase, me],
            device_id={"ctx": peer}, device_id_type=MESH,
        )

    def send_all(phase, source, dst):
        def body(k, _):
            peer = lax.rem(me + k, n)
            remote(phase, source(peer), dst.at[me], peer).start()
            return 0

        lax.fori_loop(1, n, body, 0)

    def wait_all(phase, source, dst):
        def body(k, _):
            peer = lax.rem(me + k, n)
            pltpu.make_async_remote_copy(
                src_ref=source(peer), dst_ref=dst.at[peer],
                send_sem=send_sem.at[phase, peer], recv_sem=recv_sem.at[phase, peer],
                device_id={"ctx": peer}, device_id_type=MESH,
            ).wait()
            return 0

        lax.fori_loop(1, n, body, 0)

    q_chunks = ql // LANES
    kv_chunks = -(-kvw // LANES)
    chunks = q_chunks + kv_chunks
    s1[...] = jnp.zeros_like(s1)
    x = hidden[...]
    arrive(l_qd)
    q_part = dot(x, v_qd[...])
    arrive(l_kd)
    kv_part = dot(x, v_kd[...])
    for c in range(chunks):
        d, s = c % n, c // n
        where = pl.ds(s * rows, rows)
        if c < q_chunks:
            s1[d, where, :] = q_part[:, c * LANES:(c + 1) * LANES]
        else:
            begin = (c - q_chunks) * LANES
            width = min(LANES, kvw - begin)
            s1[d, where, :width] = kv_part[:, begin:begin + width]
    r1[me] = s1[me]
    pl.semaphore_wait(barrier, n - 1)
    send_all(0, lambda peer: s1.at[peer], r1)

    tokens = cache.shape[1]
    token = lax.broadcasted_iota(jnp.int32, (1, tokens), 1)
    position = me * tokens + token
    block_of = position // BLOCK
    used = []
    for r in range(rows):
        hit = block_of == blocks[r, 0]
        for k in range(1, blocks.shape[1]):
            hit = hit | (block_of == blocks[r, k])
        used.append(jnp.where(hit & (position < lengths[r]), 1.0, 0.0))
    used = jnp.concatenate(used, axis=1)
    row_of_token = lax.broadcasted_iota(jnp.int32, (n * pad, rows * tokens), 1) // tokens
    row_of_query = lax.broadcasted_iota(jnp.int32, (n * pad, rows * tokens), 0) % rows
    valid = (row_of_token == row_of_query) & (used > 0.5)
    if pad > kr:
        qs[...] = jnp.zeros_like(qs)

    wait_all(0, lambda peer: s1.at[peer], r1)
    g2[me] = jnp.sum(r1[...], axis=0)
    send_all(1, lambda peer: g2.at[me], g2)
    wait_all(1, lambda peer: g2.at[me], g2)

    def chunk(c):
        return g2[c % n, pl.ds((c // n) * rows, rows), :]

    q_low = jnp.concatenate([chunk(c) for c in range(q_chunks)], axis=1)
    kv_new = jnp.concatenate([chunk(c) for c in range(q_chunks, chunks)], axis=1)[:, :kvw]
    q_mean = jnp.sum(q_low * q_low, axis=1, keepdims=True) * (1.0 / ql)
    q_normed = (q_low * lax.rsqrt(q_mean + 1e-06) * q_gain[...]).astype(BF16)
    arrive(l_qu)
    qf[...] = dot(q_normed, v_qu[...]).astype(BF16).astype(F32)
    arrive(l_uk)
    for h in range(heads):
        nope = qf[:, h * head_width:h * head_width + NOPE].astype(BF16)
        where = pl.ds(h * rows, rows)
        qs[where, :lat] = dot(nope, v_uk[h])
        qs[where, lat:] = qf[:, h * head_width + NOPE:(h + 1) * head_width]
    query = qs[...].astype(BF16)
    qall[me] = query
    send_all(2, lambda peer: qall.at[me], qall)

    kv_lat = kv_new[:, :lat]
    kv_mean = jnp.sum(kv_lat * kv_lat, axis=1, keepdims=True) * (1.0 / lat)
    lat_new = kv_lat * lax.rsqrt(kv_mean + 1e-06) * kv_gain[...]
    key_new = jnp.concatenate([lat_new, kv_new[:, lat:]], axis=1).astype(BF16).astype(F32)
    own_row = lax.broadcasted_iota(jnp.int32, (pad, kvw), 0) % rows
    key_rows = jnp.broadcast_to(key_new[0:1], (pad, kvw))
    for r in range(1, rows):
        key_rows = jnp.where(own_row == r, jnp.broadcast_to(key_new[r:r + 1], (pad, kvw)), key_rows)
    own = scale * jnp.sum(query.astype(F32) * key_rows, axis=1, keepdims=True)

    arrive(l_ca)
    wait_all(2, lambda peer: qall.at[me], qall)
    q_mat = qall[...].reshape(n * pad, kvw)
    c_mat = v_ca[...].reshape(rows * tokens, kvw)
    score = scale * lax.dot_general(
        q_mat, c_mat, (((1,), (1,)), ((), ())), preferred_element_type=F32
    )
    peak = jnp.max(jnp.where(valid, score, -1e30), axis=1, keepdims=True)
    expo = jnp.where(valid, jnp.exp(score - peak), 0.0)
    total = jnp.sum(expo, axis=1, keepdims=True)
    numer = dot(expo.astype(BF16), c_mat[:, :lat])
    s4[:, :, :lat] = numer.astype(BF16).reshape(n, pad, lat)
    lane = lax.broadcasted_iota(jnp.int32, (n * pad, LANES), 1)
    stats = jnp.zeros((n * pad, LANES), F32)
    for place, piece in enumerate(split3(peak) + split3(total)):
        stats = jnp.where(lane == place, piece, stats)
    s4[:, :, lat:] = stats.astype(BF16).reshape(n, pad, LANES)
    send_all(3, lambda peer: s4.at[peer], r4)
    r4[me] = s4[me]
    wait_all(3, lambda peer: s4.at[peer], r4)

    got = r4[:, :, lat:].astype(F32)
    peaks = got[:, :, 0:1] + got[:, :, 1:2] + got[:, :, 2:3]
    totals = got[:, :, 3:4] + got[:, :, 4:5] + got[:, :, 5:6]
    top = jnp.maximum(jnp.max(peaks, axis=0), own)
    factor = jnp.exp(peaks - top[None])
    own_weight = jnp.exp(own - top)
    denom = jnp.sum(totals * factor, axis=0) + own_weight
    mixed = own_weight * key_rows[:, :lat]
    for d in range(n):
        mixed = mixed + factor[d] * r4[d, :, :lat].astype(F32)
    latent = (mixed / denom).astype(BF16).astype(F32)
    arrive(l_uv)
    head_out = jnp.concatenate(
        [dot(latent[h * rows:(h + 1) * rows].astype(BF16), v_uv[h]) for h in range(heads)], axis=1
    ).astype(BF16)

    arrive(l_op)
    width = out.shape[1]
    group = math.lcm(width, LANES)
    for g in range(n * width // group):
        part = dot(head_out, v_op[:, g * group:(g + 1) * group])
        for i in range(group // width):
            d = g * (group // width) + i
            s5[d] = part[:, i * width:(i + 1) * width]

            @pl.when(me != d)
            def _():
                remote(4, s5.at[d], r5.at[me], d).start()

    r5[me] = s5[me]
    wait_all(4, lambda peer: s5.at[peer], r5)
    out[...] = jnp.sum(r5[...], axis=0).astype(BF16)


def solution(mesh):
    n = mesh.shape["ctx"]

    def per_device(
        hidden, q_down, q_gain, q_up, w_uk, kv_down, kv_gain, w_uv, o_proj, cache, lengths, blocks
    ):
        rows = hidden.shape[0]
        heads, _, lat = w_uk.shape
        kvw = kv_down.shape[1]
        width = o_proj.shape[1] // n
        pad = -(-rows * heads // 16) * 16
        chunks = q_down.shape[1] // LANES + -(-kvw // LANES)
        held = -(-chunks // n) * rows
        vmem = pl.BlockSpec(memory_space=pltpu.VMEM)
        smem = pl.BlockSpec(memory_space=pltpu.SMEM)
        hbm = pl.BlockSpec(memory_space=pl.ANY)
        big = (q_down, kv_down, q_up, w_uk, cache, w_uv, o_proj)
        return pl.pallas_call(
            functools.partial(kernel, n, rows, heads, lat, pad),
            out_shape=jax.ShapeDtypeStruct((rows, width), BF16),
            in_specs=[smem, smem, vmem, vmem, vmem] + [hbm] * len(big),
            out_specs=vmem,
            scratch_shapes=[pltpu.VMEM(a.shape, a.dtype) for a in big] + [
                pltpu.VMEM((n, held, LANES), F32),
                pltpu.VMEM((n, held, LANES), F32),
                pltpu.VMEM((n, held, LANES), F32),
                pltpu.VMEM((rows, q_up.shape[1]), F32),
                pltpu.VMEM((pad, kvw), F32),
                pltpu.VMEM((n, pad, kvw), BF16),
                pltpu.VMEM((n, pad, lat + LANES), BF16),
                pltpu.VMEM((n, pad, lat + LANES), BF16),
                pltpu.VMEM((n, rows, width), F32),
                pltpu.VMEM((n, rows, width), F32),
                pltpu.SemaphoreType.DMA((17,)),
                pltpu.SemaphoreType.DMA((5, n)),
                pltpu.SemaphoreType.DMA((5, n)),
            ],
            compiler_params=pltpu.CompilerParams(
                collective_id=0, has_side_effects=True, vmem_limit_bytes=56 * 1024 * 1024
            ),
        )(lengths, blocks, hidden, q_gain[None], kv_gain[None], *big)

    placed = (
        P("grp", "ctx"),
        P("ctx", None),
        P(),
        P(None, "ctx"),
        P("ctx", None, None),
        P("ctx", None),
        P(),
        P("ctx", None, None),
        P("ctx", None),
        P("grp", "ctx", None),
        P("grp"),
        P("grp", None),
    )
    return jax.shard_map(
        per_device, mesh=mesh, in_specs=placed, out_specs=P("grp", "ctx"), check_vma=False
    )
```

time: 285 us -> 46.8 us (0.16)
  blocking collectives: 118 us -> 0 us
  waiting for transfers between devices: 103 us -> 0 us
  Pallas kernels: 0 us -> 41.9 us
  other arithmetic: 19.5 us -> 0 us
  matrix products: 18.9 us -> 0 us
  between operations: 13.5 us -> 0.01 us
  local copies, waits for them, and re-layouts: 10.4 us -> 4.66 us
    unnamed x3 -> x0, waiting for transfers between devices: 67 us -> none
    psum x1 -> x0, blocking collectives: 63 us -> none  [per_device(): q_low, kv_new = lax.psum((q_part, kv_part), 'ctx')]
    all_gather x3 -> x0, blocking collectives: 54.9 us -> none  [the longest x2 36.9 us: combined_all(): pieces = jax.tree.map(lambda part: lax.all_gather(part, axis), value)]
    pallas_call x0 -> x1, Pallas kernels: none -> 41.9 us  [per_device(): pl.pallas_call(functools.partial(kernel, n, rows, heads, lat, pad), out_s...]
    all_gather x1 -> x0, waiting for transfers between devices: 36.5 us -> none  [combined_all(): pieces = jax.tree.map(lambda part: lax.all_gather(part, axis), value)]
    add x32 -> x0, other arithmetic: 18.7 us -> none  [the longest x15 18.2 us: combine_parts(): numer = first[2] * fac_one[..., None] + second[2] * fac_two[..., None]]
    unnamed x1 -> x0, matrix products: 10.3 us -> none
    dot_general x7 -> x0, matrix products: 8.64 us -> none  [the longest x1 3.12 us: per_device(): jnp.dot(q_normed, q_up, preferred_element_type=jnp.float32)]
  transfers between devices with their start and end apart: 2 -> 0, of which waited for: 2 -> 0; matrix products, arithmetic and copies ran while one was open for 0% -> 0% of each run, Pallas kernels for 0% -> 0%
where the time goes in v1:
time: 46.8 us; the launch traced here: 46.6 us
  Pallas kernels  41.9 us (90%)
  local copies, waits for them, and re-layouts  4.66 us (10%)
    pallas_call x1, Pallas kernels, per_device(): pl.pallas_call(functools.partial(kernel, n, rows, heads, lat, pad), out_s...  41.9 us
    unnamed x2, local copies, waits for them, and re-layouts  3.39 us
    broadcast_in_dim x1, local copies, waits for them, and re-layouts, per_device(): q_gain[None]  1.28 us

profile of v1, /device:TPU:0, one launch (start us, length us, event | category | flops | bytes accessed | tf_op | source)
XLA Modules:
  0.0 46.6 jit_solution(4537029305954000925)
XLA Ops:
  0.0 1.3 %broadcast_in_dim.6.q_gain = f32[1,1536]{1,0:T(1,128)} reshape(f32[1536]{0:T(1024)} %param.14) | data formatting | bytes 12288 | tf_op jit(solution)/shard_map/broadcast_in_dim | solution.py:278
  1.3 2.1 %copy.13.cache = bf16[2,256,576]{2,1,0:T(8,128)(2,1)} copy(bf16[2,256,576]{1,2,0:T(8,128)(2,1)} %param.21) | data formatting | bytes 1179648 | tf_op args[9]
  3.4 41.9 %shard_map.118 = bf16[2,448]{1,0:T(2,128)(2,1)} custom-call(s32[2]{0:T(128)} %lengths.1, s32[2,32]{1,0:T(2,128)} %blocks.1, bf16[2,448]{1,0:T(2,128)(2,1)} %hidden.1, f32[1,1536]{1,0:T(1,128)} %broadcast_in_dim.6.q_gain, f32[1,512]{1,0:T(1,128)} %bitcast.1, bf16[448,1536]{1,0:T(8,128)(2,1)} %q_down.1, bf16[448,576]{1,0:T(8,128)(2,1)} %kv_down.1, ...), custom_call_target="tpu_custom_call" | custom-call | tf_op jit(solution)/shard_map/pallas_call | solution.py:255
  45.3 1.3 %copy.15 = bf16[2,448]{1,0:T(2,128)(2,1)} copy(bf16[2,448]{1,0:T(2,128)(2,1)} %shard_map.118) | data formatting | bytes 3584

commit v2 on v1

--- a/solution.py
+++ b/solution.py
@@ -10,6 +10,7 @@
 
 NOPE = 128
 ROPE = 64
+PAIR = 2
 BLOCK = 64
 LANES = 128
 F32 = jnp.float32
@@ -34,7 +35,7 @@
     out,
     v_qd, v_kd, v_qu, v_uk, v_ca, v_uv, v_op,
     s1, r1, g2, qf, qs, qall, s4, r4, s5, r5,
-    load_sem, send_sem, recv_sem,
+    load_sem, pair_sem, send_sem, recv_sem,
 ):
     me = lax.axis_index("ctx")
     ql = q_down.shape[1]
@@ -62,7 +63,8 @@
     l_kd = load(kv_down, v_kd)
     l_qu = load(q_up, v_qu, 4)
     l_uk = load(w_uk, v_uk)
-    l_ca = load(cache, v_ca)
+    core = lax.rem(me, PAIR)
+    l_ca = load(cache, v_ca.at[core])
     l_uv = load(w_uv, v_uv)
     l_op = load(o_proj, v_op, 8)
 
@@ -80,32 +82,35 @@
 
     lax.fori_loop(1, n, greet, 0)
 
-    def remote(phase, src, dst, peer):
+    everyone = (n, me, lambda index: index)
+    alike = (n // PAIR, me // PAIR, lambda index: index * PAIR + core)
+
+    def remote(phase, src, dst, peer, slot, device):
         return pltpu.make_async_remote_copy(
             src_ref=src, dst_ref=dst,
-            send_sem=send_sem.at[phase, peer], recv_sem=recv_sem.at[phase, me],
-            device_id={"ctx": peer}, device_id_type=MESH,
+            send_sem=send_sem.at[phase, peer], recv_sem=recv_sem.at[phase, slot],
+            device_id={"ctx": device}, device_id_type=MESH,
         )
 
-    def send_all(phase, source, dst):
+    def send_all(phase, team, source, dst):
+        size, mine, device = team
+
         def body(k, _):
-            peer = lax.rem(me + k, n)
-            remote(phase, source(peer), dst.at[me], peer).start()
+            peer = lax.rem(mine + k, size)
+            remote(phase, source(peer), dst.at[mine], peer, mine, device(peer)).start()
             return 0
 
-        lax.fori_loop(1, n, body, 0)
-
-    def wait_all(phase, source, dst):
+        lax.fori_loop(1, size, body, 0)
+
+    def wait_all(phase, team, source, dst):
+        size, mine, device = team
+
         def body(k, _):
-            peer = lax.rem(me + k, n)
-            pltpu.make_async_remote_copy(
-                src_ref=source(peer), dst_ref=dst.at[peer],
-                send_sem=send_sem.at[phase, peer], recv_sem=recv_sem.at[phase, peer],
-                device_id={"ctx": peer}, device_id_type=MESH,
-            ).wait()
+            peer = lax.rem(mine + k, size)
+            remote(phase, source(peer), dst.at[peer], peer, peer, device(peer)).wait()
             return 0
 
-        lax.fori_loop(1, n, body, 0)
+        lax.fori_loop(1, size, body, 0)
 
     q_chunks = ql // LANES
     kv_chunks = -(-kvw // LANES)
@@ -127,11 +132,17 @@
             s1[d, where, :width] = kv_part[:, begin:begin + width]
     r1[me] = s1[me]
     pl.semaphore_wait(barrier, n - 1)
-    send_all(0, lambda peer: s1.at[peer], r1)
-
-    tokens = cache.shape[1]
-    token = lax.broadcasted_iota(jnp.int32, (1, tokens), 1)
-    position = me * tokens + token
+    send_all(0, everyone, lambda peer: s1.at[peer], r1)
+    partner = me + 1 - 2 * core
+    share = pltpu.make_async_remote_copy(
+        src_ref=cache, dst_ref=v_ca.at[core], send_sem=pair_sem.at[0], recv_sem=pair_sem.at[1],
+        device_id={"ctx": partner}, device_id_type=MESH,
+    )
+    share.start()
+
+    tokens = cache.shape[2]
+    token = lax.broadcasted_iota(jnp.int32, (1, PAIR * tokens), 1)
+    position = (me - core) * tokens + token
     block_of = position // BLOCK
     used = []
     for r in range(rows):
@@ -140,16 +151,17 @@
             hit = hit | (block_of == blocks[r, k])
         used.append(jnp.where(hit & (position < lengths[r]), 1.0, 0.0))
     used = jnp.concatenate(used, axis=1)
-    row_of_token = lax.broadcasted_iota(jnp.int32, (n * pad, rows * tokens), 1) // tokens
-    row_of_query = lax.broadcasted_iota(jnp.int32, (n * pad, rows * tokens), 0) % rows
+    shape = (n // PAIR * pad, rows * PAIR * tokens)
+    row_of_token = lax.broadcasted_iota(jnp.int32, shape, 1) // (PAIR * tokens)
+    row_of_query = lax.broadcasted_iota(jnp.int32, shape, 0) % rows
     valid = (row_of_token == row_of_query) & (used > 0.5)
     if pad > kr:
         qs[...] = jnp.zeros_like(qs)
 
-    wait_all(0, lambda peer: s1.at[peer], r1)
+    wait_all(0, everyone, lambda peer: s1.at[peer], r1)
     g2[me] = jnp.sum(r1[...], axis=0)
-    send_all(1, lambda peer: g2.at[me], g2)
-    wait_all(1, lambda peer: g2.at[me], g2)
+    send_all(1, everyone, lambda peer: g2.at[me], g2)
+    wait_all(1, everyone, lambda peer: g2.at[me], g2)
 
     def chunk(c):
         return g2[c % n, pl.ds((c // n) * rows, rows), :]
@@ -157,7 +169,8 @@
     q_low = jnp.concatenate([chunk(c) for c in range(q_chunks)], axis=1)
     kv_new = jnp.concatenate([chunk(c) for c in range(q_chunks, chunks)], axis=1)[:, :kvw]
     q_mean = jnp.sum(q_low * q_low, axis=1, keepdims=True) * (1.0 / ql)
-    q_normed = (q_low * lax.rsqrt(q_mean + 1e-06) * q_gain[...]).astype(BF16)
+    gain = jnp.concatenate([q_gain[c:c + 1, :] for c in range(q_chunks)], axis=1)
+    q_normed = (q_low * lax.rsqrt(q_mean + 1e-06) * gain).astype(BF16)
     arrive(l_qu)
     qf[...] = dot(q_normed, v_qu[...]).astype(BF16).astype(F32)
     arrive(l_uk)
@@ -167,8 +180,8 @@
         qs[where, :lat] = dot(nope, v_uk[h])
         qs[where, lat:] = qf[:, h * head_width + NOPE:(h + 1) * head_width]
     query = qs[...].astype(BF16)
-    qall[me] = query
-    send_all(2, lambda peer: qall.at[me], qall)
+    qall[me // PAIR] = query
+    send_all(2, alike, lambda peer: qall.at[me // PAIR], qall)
 
     kv_lat = kv_new[:, :lat]
     kv_mean = jnp.sum(kv_lat * kv_lat, axis=1, keepdims=True) * (1.0 / lat)
@@ -181,25 +194,33 @@
     own = scale * jnp.sum(query.astype(F32) * key_rows, axis=1, keepdims=True)
 
     arrive(l_ca)
-    wait_all(2, lambda peer: qall.at[me], qall)
-    q_mat = qall[...].reshape(n * pad, kvw)
-    c_mat = v_ca[...].reshape(rows * tokens, kvw)
-    score = scale * lax.dot_general(
-        q_mat, c_mat, (((1,), (1,)), ((), ())), preferred_element_type=F32
-    )
+    pltpu.make_async_remote_copy(
+        src_ref=cache, dst_ref=v_ca.at[1 - core], send_sem=pair_sem.at[0], recv_sem=pair_sem.at[1],
+        device_id={"ctx": partner}, device_id_type=MESH,
+    ).wait()
+    wait_all(2, alike, lambda peer: qall.at[me // PAIR], qall)
+    q_mat = qall[...].reshape(n // PAIR * pad, kvw)
+    parts = [(half, r) for r in range(rows) for half in range(PAIR)]
+    score = scale * jnp.concatenate([dot(q_mat, v_ca[half, r]) for half, r in parts], axis=1)
     peak = jnp.max(jnp.where(valid, score, -1e30), axis=1, keepdims=True)
     expo = jnp.where(valid, jnp.exp(score - peak), 0.0)
     total = jnp.sum(expo, axis=1, keepdims=True)
-    numer = dot(expo.astype(BF16), c_mat[:, :lat])
-    s4[:, :, :lat] = numer.astype(BF16).reshape(n, pad, lat)
-    lane = lax.broadcasted_iota(jnp.int32, (n * pad, LANES), 1)
-    stats = jnp.zeros((n * pad, LANES), F32)
+    weights = expo.astype(BF16)
+    numer = jnp.zeros((n // PAIR * pad, lat), F32)
+    for place, (half, r) in enumerate(parts):
+        numer = numer + lax.dot_general(
+            weights[:, place * tokens:(place + 1) * tokens], v_ca[half, r, :lat, :],
+            (((1,), (1,)), ((), ())), preferred_element_type=F32,
+        )
+    s4[:, :, :lat] = numer.astype(BF16).reshape(n // PAIR, pad, lat)
+    lane = lax.broadcasted_iota(jnp.int32, (n // PAIR * pad, LANES), 1)
+    stats = jnp.zeros((n // PAIR * pad, LANES), F32)
     for place, piece in enumerate(split3(peak) + split3(total)):
         stats = jnp.where(lane == place, piece, stats)
-    s4[:, :, lat:] = stats.astype(BF16).reshape(n, pad, LANES)
-    send_all(3, lambda peer: s4.at[peer], r4)
-    r4[me] = s4[me]
-    wait_all(3, lambda peer: s4.at[peer], r4)
+    s4[:, :, lat:] = stats.astype(BF16).reshape(n // PAIR, pad, LANES)
+    send_all(3, alike, lambda peer: s4.at[peer], r4)
+    r4[me // PAIR] = s4[me // PAIR]
+    wait_all(3, alike, lambda peer: s4.at[peer], r4)
 
     got = r4[:, :, lat:].astype(F32)
     peaks = got[:, :, 0:1] + got[:, :, 1:2] + got[:, :, 2:3]
@@ -209,7 +230,7 @@
     own_weight = jnp.exp(own - top)
     denom = jnp.sum(totals * factor, axis=0) + own_weight
     mixed = own_weight * key_rows[:, :lat]
-    for d in range(n):
+    for d in range(n // PAIR):
         mixed = mixed + factor[d] * r4[d, :, :lat].astype(F32)
     latent = (mixed / denom).astype(BF16).astype(F32)
     arrive(l_uv)
@@ -219,7 +240,7 @@
 
     arrive(l_op)
     width = out.shape[1]
-    group = math.lcm(width, LANES)
+    group = math.lcm(width, 2 * LANES)
     for g in range(n * width // group):
         part = dot(head_out, v_op[:, g * group:(g + 1) * group])
         for i in range(group // width):
@@ -228,10 +249,10 @@
 
             @pl.when(me != d)
             def _():
-                remote(4, s5.at[d], r5.at[me], d).start()
+                remote(4, s5.at[d], r5.at[me], d, me, d).start()
 
     r5[me] = s5[me]
-    wait_all(4, lambda peer: s5.at[peer], r5)
+    wait_all(4, everyone, lambda peer: s5.at[peer], r5)
     out[...] = jnp.sum(r5[...], axis=0).astype(BF16)
 
 
@@ -251,31 +272,35 @@
         vmem = pl.BlockSpec(memory_space=pltpu.VMEM)
         smem = pl.BlockSpec(memory_space=pltpu.SMEM)
         hbm = pl.BlockSpec(memory_space=pl.ANY)
+        cache = jnp.swapaxes(cache, 1, 2)
         big = (q_down, kv_down, q_up, w_uk, cache, w_uv, o_proj)
+        held_in = [a.shape for a in big]
+        held_in[4] = (PAIR,) + cache.shape
         return pl.pallas_call(
             functools.partial(kernel, n, rows, heads, lat, pad),
             out_shape=jax.ShapeDtypeStruct((rows, width), BF16),
             in_specs=[smem, smem, vmem, vmem, vmem] + [hbm] * len(big),
             out_specs=vmem,
-            scratch_shapes=[pltpu.VMEM(a.shape, a.dtype) for a in big] + [
+            scratch_shapes=[pltpu.VMEM(shape, BF16) for shape in held_in] + [
                 pltpu.VMEM((n, held, LANES), F32),
                 pltpu.VMEM((n, held, LANES), F32),
                 pltpu.VMEM((n, held, LANES), F32),
                 pltpu.VMEM((rows, q_up.shape[1]), F32),
                 pltpu.VMEM((pad, kvw), F32),
-                pltpu.VMEM((n, pad, kvw), BF16),
-                pltpu.VMEM((n, pad, lat + LANES), BF16),
-                pltpu.VMEM((n, pad, lat + LANES), BF16),
+                pltpu.VMEM((n // PAIR, pad, kvw), BF16),
+                pltpu.VMEM((n // PAIR, pad, lat + LANES), BF16),
+                pltpu.VMEM((n // PAIR, pad, lat + LANES), BF16),
                 pltpu.VMEM((n, rows, width), F32),
                 pltpu.VMEM((n, rows, width), F32),
                 pltpu.SemaphoreType.DMA((17,)),
+                pltpu.SemaphoreType.DMA((2,)),
                 pltpu.SemaphoreType.DMA((5, n)),
                 pltpu.SemaphoreType.DMA((5, n)),
             ],
             compiler_params=pltpu.CompilerParams(
                 collective_id=0, has_side_effects=True, vmem_limit_bytes=56 * 1024 * 1024
             ),
-        )(lengths, blocks, hidden, q_gain[None], kv_gain[None], *big)
+        )(lengths, blocks, hidden, q_gain.reshape(-1, LANES), kv_gain[None], *big)
 
     placed = (
         P("grp", "ctx"),

time: 46.8 us -> 36.8 us (0.79)
  Pallas kernels: 41.9 us -> 35.3 us
  local copies, waits for them, and re-layouts: 4.66 us -> 1.26 us
    pallas_call x1, Pallas kernels: 41.9 us -> 35.3 us  [per_device(): pl.pallas_call(functools.partial(kernel, n, rows, heads, lat, pad), out_s...]
    unnamed x2 -> x1, local copies, waits for them, and re-layouts: 3.39 us -> 1.26 us
    broadcast_in_dim x1 -> x0, local copies, waits for them, and re-layouts: 1.28 us -> none  [per_device(): q_gain[None]]
where the time goes in v2:
time: 36.8 us; the launch traced here: 36.6 us
  Pallas kernels  35.3 us (96%)
  local copies, waits for them, and re-layouts  1.26 us (3%)
    pallas_call x1, Pallas kernels, per_device(): pl.pallas_call(functools.partial(kernel, n, rows, heads, lat, pad), out_s...  35.3 us
    unnamed x1, local copies, waits for them, and re-layouts  1.26 us

profile of v2, /device:TPU:0, one launch (start us, length us, event | category | flops | bytes accessed | tf_op | source)
XLA Modules:
  0.0 36.6 jit_solution(13164485356906056475)
XLA Ops:
  0.0 35.3 %shard_map.118 = bf16[2,448]{1,0:T(2,128)(2,1)} custom-call(s32[2]{0:T(128)} %lengths.1, s32[2,32]{1,0:T(2,128)} %blocks.1, bf16[2,448]{1,0:T(2,128)(2,1)} %hidden.1, f32[12,128]{1,0:T(8,128)} %bitcast.4, f32[1,512]{1,0:T(1,128)} %bitcast.5, bf16[448,1536]{1,0:T(8,128)(2,1)} %q_down.1, bf16[448,576]{1,0:T(8,128)(2,1)} %kv_down.1, bf16[1536,1536]{1,0:T(8,128)(2,1)} %q_up.1, ...), custom_call_target="tpu_custom_call" | custom-call | tf_op jit(solution)/shard_map/pallas_call | solution.py:279
  35.4 1.3 %copy.14 = bf16[2,448]{1,0:T(2,128)(2,1)} copy(bf16[2,448]{1,0:T(2,128)(2,1)} %shard_map.118) | data formatting | bytes 3584

commit v3 on v2

--- a/solution.py
+++ b/solution.py
@@ -72,45 +72,44 @@
         for copy in copies:
             copy.wait()
 
-    barrier = pltpu.get_barrier_semaphore()
-
-    def greet(k, _):
-        pl.semaphore_signal(
-            barrier, inc=1, device_id={"ctx": lax.rem(me + k, n)}, device_id_type=MESH
-        )
-        return 0
-
-    lax.fori_loop(1, n, greet, 0)
-
     everyone = (n, me, lambda index: index)
     alike = (n // PAIR, me // PAIR, lambda index: index * PAIR + core)
 
-    def remote(phase, src, dst, peer, slot, device):
+    def remote(phase, src, dst, device):
         return pltpu.make_async_remote_copy(
-            src_ref=src, dst_ref=dst,
-            send_sem=send_sem.at[phase, peer], recv_sem=recv_sem.at[phase, slot],
+            src_ref=src, dst_ref=dst, send_sem=send_sem.at[phase], recv_sem=recv_sem.at[phase],
             device_id={"ctx": device}, device_id_type=MESH,
         )
 
+    def around(mine, k, size):
+        peer = mine + k
+        return jnp.where(peer >= size, peer - size, peer)
+
+    def for_peers(team, body):
+        size, mine, _ = team
+        if size <= 16:
+            for k in range(1, size):
+                body(around(mine, k, size))
+        else:
+            lax.fori_loop(1, size, lambda k, _: (body(around(mine, k, size)), 0)[1], 0)
+
+    barrier = pltpu.get_barrier_semaphore()
+    for_peers(everyone, lambda peer: pl.semaphore_signal(
+        barrier, inc=1, device_id={"ctx": peer}, device_id_type=MESH
+    ))
+
     def send_all(phase, team, source, dst):
-        size, mine, device = team
-
-        def body(k, _):
-            peer = lax.rem(mine + k, size)
-            remote(phase, source(peer), dst.at[mine], peer, mine, device(peer)).start()
-            return 0
-
-        lax.fori_loop(1, size, body, 0)
-
-    def wait_all(phase, team, source, dst):
-        size, mine, device = team
-
-        def body(k, _):
-            peer = lax.rem(mine + k, size)
-            remote(phase, source(peer), dst.at[peer], peer, peer, device(peer)).wait()
-            return 0
-
-        lax.fori_loop(1, size, body, 0)
+        _, mine, device = team
+        for_peers(
+            team, lambda peer: remote(phase, source(peer), dst.at[mine], device(peer)).start()
+        )
+
+    def whole(phase, team, dst):
+        view = dst.at[pl.ds(0, team[0] - 1)]
+        return remote(phase, view, view, around(me, 1, n))
+
+    def wait_all(phase, team, dst):
+        whole(phase, team, dst).wait_recv()
 
     q_chunks = ql // LANES
     kv_chunks = -(-kvw // LANES)
@@ -158,10 +157,10 @@
     if pad > kr:
         qs[...] = jnp.zeros_like(qs)
 
-    wait_all(0, everyone, lambda peer: s1.at[peer], r1)
+    wait_all(0, everyone, r1)
     g2[me] = jnp.sum(r1[...], axis=0)
     send_all(1, everyone, lambda peer: g2.at[me], g2)
-    wait_all(1, everyone, lambda peer: g2.at[me], g2)
+    wait_all(1, everyone, g2)
 
     def chunk(c):
         return g2[c % n, pl.ds((c // n) * rows, rows), :]
@@ -198,7 +197,7 @@
         src_ref=cache, dst_ref=v_ca.at[1 - core], send_sem=pair_sem.at[0], recv_sem=pair_sem.at[1],
         device_id={"ctx": partner}, device_id_type=MESH,
     ).wait()
-    wait_all(2, alike, lambda peer: qall.at[me // PAIR], qall)
+    wait_all(2, alike, qall)
     q_mat = qall[...].reshape(n // PAIR * pad, kvw)
     parts = [(half, r) for r in range(rows) for half in range(PAIR)]
     score = scale * jnp.concatenate([dot(q_mat, v_ca[half, r]) for half, r in parts], axis=1)
@@ -220,7 +219,7 @@
     s4[:, :, lat:] = stats.astype(BF16).reshape(n // PAIR, pad, LANES)
     send_all(3, alike, lambda peer: s4.at[peer], r4)
     r4[me // PAIR] = s4[me // PAIR]
-    wait_all(3, alike, lambda peer: s4.at[peer], r4)
+    wait_all(3, alike, r4)
 
     got = r4[:, :, lat:].astype(F32)
     peaks = got[:, :, 0:1] + got[:, :, 1:2] + got[:, :, 2:3]
@@ -249,11 +248,15 @@
 
             @pl.when(me != d)
             def _():
-                remote(4, s5.at[d], r5.at[me], d, me, d).start()
+                remote(4, s5.at[d], r5.at[me], d).start()
 
     r5[me] = s5[me]
-    wait_all(4, everyone, lambda peer: s5.at[peer], r5)
+    wait_all(4, everyone, r5)
     out[...] = jnp.sum(r5[...], axis=0).astype(BF16)
+    for phase, team, dst in (
+        (0, everyone, r1), (1, everyone, g2), (2, alike, qall), (3, alike, r4), (4, everyone, r5)
+    ):
+        whole(phase, team, dst).wait_send()
 
 
 def solution(mesh):
@@ -294,8 +297,8 @@
                 pltpu.VMEM((n, rows, width), F32),
                 pltpu.SemaphoreType.DMA((17,)),
                 pltpu.SemaphoreType.DMA((2,)),
-                pltpu.SemaphoreType.DMA((5, n)),
-                pltpu.SemaphoreType.DMA((5, n)),
+                pltpu.SemaphoreType.DMA((5,)),
+                pltpu.SemaphoreType.DMA((5,)),
             ],
             compiler_params=pltpu.CompilerParams(
                 collective_id=0, has_side_effects=True, vmem_limit_bytes=56 * 1024 * 1024

time: 36.8 us -> 34.8 us (0.946)
  Pallas kernels: 35.3 us -> 33.4 us
    pallas_call x1, Pallas kernels: 35.3 us -> 33.4 us  [per_device(): pl.pallas_call(functools.partial(kernel, n, rows, heads, lat, pad), out_s...]
where the time goes in v3:
time: 34.8 us; the launch traced here: 34.6 us
  Pallas kernels  33.4 us (96%)
  local copies, waits for them, and re-layouts  1.26 us (4%)
    pallas_call x1, Pallas kernels, per_device(): pl.pallas_call(functools.partial(kernel, n, rows, heads, lat, pad), out_s...  33.4 us
    unnamed x1, local copies, waits for them, and re-layouts  1.26 us

profile of v3, /device:TPU:0, one launch (start us, length us, event | category | flops | bytes accessed | tf_op | source)
XLA Modules:
  0.0 34.6 jit_solution(2340445288593243411)
XLA Ops:
  0.0 33.4 %shard_map.118 = bf16[2,448]{1,0:T(2,128)(2,1)} custom-call(s32[2]{0:T(128)} %lengths.1, s32[2,32]{1,0:T(2,128)} %blocks.1, bf16[2,448]{1,0:T(2,128)(2,1)} %hidden.1, f32[12,128]{1,0:T(8,128)} %bitcast.4, f32[1,512]{1,0:T(1,128)} %bitcast.5, bf16[448,1536]{1,0:T(8,128)(2,1)} %q_down.1, bf16[448,576]{1,0:T(8,128)(2,1)} %kv_down.1, bf16[1536,1536]{1,0:T(8,128)(2,1)} %q_up.1, ...), custom_call_target="tpu_custom_call" | custom-call | tf_op jit(solution)/shard_map/pallas_call | solution.py:282
  33.4 1.3 %copy.14 = bf16[2,448]{1,0:T(2,128)(2,1)} copy(bf16[2,448]{1,0:T(2,128)(2,1)} %shard_map.118) | data formatting | bytes 3584

commit v4 on v3

--- a/solution.py
+++ b/solution.py
@@ -33,7 +33,7 @@
     lengths, blocks, hidden, q_gain, kv_gain,
     q_down, kv_down, q_up, w_uk, cache, w_uv, o_proj,
     out,
-    v_qd, v_kd, v_qu, v_uk, v_ca, v_uv, v_op,
+    v_qd, v_kd, v_qu, v_uk, v_ca, v_uv, v_op, v_ct,
     s1, r1, g2, qf, qs, qall, s4, r4, s5, r5,
     load_sem, pair_sem, send_sem, recv_sem,
 ):
@@ -150,7 +150,10 @@
             hit = hit | (block_of == blocks[r, k])
         used.append(jnp.where(hit & (position < lengths[r]), 1.0, 0.0))
     used = jnp.concatenate(used, axis=1)
-    shape = (n // PAIR * pad, rows * PAIR * tokens)
+    size = n // PAIR
+    mine = me // PAIR
+    cut = (size + 1) // 2
+    shape = (cut * pad, rows * PAIR * tokens)
     row_of_token = lax.broadcasted_iota(jnp.int32, shape, 1) // (PAIR * tokens)
     row_of_query = lax.broadcasted_iota(jnp.int32, shape, 0) % rows
     valid = (row_of_token == row_of_query) & (used > 0.5)
@@ -179,8 +182,10 @@
         qs[where, :lat] = dot(nope, v_uk[h])
         qs[where, lat:] = qf[:, h * head_width + NOPE:(h + 1) * head_width]
     query = qs[...].astype(BF16)
-    qall[me // PAIR] = query
-    send_all(2, alike, lambda peer: qall.at[me // PAIR], qall)
+    qall[0] = query
+    for k in range(1, size):
+        device = alike[2](around(mine, k, size))
+        remote(2 if k < cut else 3, qall.at[0], qall.at[k], device).start()
 
     kv_lat = kv_new[:, :lat]
     kv_mean = jnp.sum(kv_lat * kv_lat, axis=1, keepdims=True) * (1.0 / lat)
@@ -197,29 +202,36 @@
         src_ref=cache, dst_ref=v_ca.at[1 - core], send_sem=pair_sem.at[0], recv_sem=pair_sem.at[1],
         device_id={"ctx": partner}, device_id_type=MESH,
     ).wait()
-    wait_all(2, alike, qall)
-    q_mat = qall[...].reshape(n // PAIR * pad, kvw)
     parts = [(half, r) for r in range(rows) for half in range(PAIR)]
-    score = scale * jnp.concatenate([dot(q_mat, v_ca[half, r]) for half, r in parts], axis=1)
-    peak = jnp.max(jnp.where(valid, score, -1e30), axis=1, keepdims=True)
-    expo = jnp.where(valid, jnp.exp(score - peak), 0.0)
-    total = jnp.sum(expo, axis=1, keepdims=True)
-    weights = expo.astype(BF16)
-    numer = jnp.zeros((n // PAIR * pad, lat), F32)
     for place, (half, r) in enumerate(parts):
-        numer = numer + lax.dot_general(
-            weights[:, place * tokens:(place + 1) * tokens], v_ca[half, r, :lat, :],
-            (((1,), (1,)), ((), ())), preferred_element_type=F32,
-        )
-    s4[:, :, :lat] = numer.astype(BF16).reshape(n // PAIR, pad, lat)
-    lane = lax.broadcasted_iota(jnp.int32, (n // PAIR * pad, LANES), 1)
-    stats = jnp.zeros((n // PAIR * pad, LANES), F32)
-    for place, piece in enumerate(split3(peak) + split3(total)):
-        stats = jnp.where(lane == place, piece, stats)
-    s4[:, :, lat:] = stats.astype(BF16).reshape(n // PAIR, pad, LANES)
-    send_all(3, alike, lambda peer: s4.at[peer], r4)
-    r4[me // PAIR] = s4[me // PAIR]
-    wait_all(3, alike, r4)
+        v_ct[place * tokens:(place + 1) * tokens, :] = v_ca[half, r, :lat, :].T
+
+    def arrived(phase, ref, begin, count):
+        view = ref.at[pl.ds(begin, count)]
+        return remote(phase, view, view, around(me, 1, n))
+
+    stages = [(2, 0, cut), (3, cut, size - cut)]
+    for phase, begin, count in stages:
+        skip = 1 if begin == 0 else 0
+        arrived(phase, qall, begin + skip, count - skip).wait_recv()
+        q_mat = qall[begin:begin + count].reshape(count * pad, kvw)
+        score = scale * jnp.concatenate([dot(q_mat, v_ca[half, r]) for half, r in parts], axis=1)
+        here = valid[:count * pad]
+        peak = jnp.max(jnp.where(here, score, -1e30), axis=1, keepdims=True)
+        expo = jnp.where(here, jnp.exp(score - peak), 0.0)
+        total = jnp.sum(expo, axis=1, keepdims=True)
+        numer = dot(expo.astype(BF16), v_ct[...])
+        s4[begin:begin + count, :, :lat] = numer.astype(BF16).reshape(count, pad, lat)
+        lane = lax.broadcasted_iota(jnp.int32, (count * pad, LANES), 1)
+        stats = jnp.zeros((count * pad, LANES), F32)
+        for place, piece in enumerate(split3(peak) + split3(total)):
+            stats = jnp.where(lane == place, piece, stats)
+        s4[begin:begin + count, :, lat:] = stats.astype(BF16).reshape(count, pad, LANES)
+        for k in range(begin + skip, begin + count):
+            device = alike[2](around(mine, size - k, size))
+            remote(4, s4.at[k], r4.at[k], device).start()
+    r4[0] = s4[0]
+    wait_all(4, alike, r4)
 
     got = r4[:, :, lat:].astype(F32)
     peaks = got[:, :, 0:1] + got[:, :, 1:2] + got[:, :, 2:3]
@@ -248,15 +260,18 @@
 
             @pl.when(me != d)
             def _():
-                remote(4, s5.at[d], r5.at[me], d).start()
+                remote(5, s5.at[d], r5.at[me], d).start()
 
     r5[me] = s5[me]
-    wait_all(4, everyone, r5)
+    wait_all(5, everyone, r5)
     out[...] = jnp.sum(r5[...], axis=0).astype(BF16)
     for phase, team, dst in (
-        (0, everyone, r1), (1, everyone, g2), (2, alike, qall), (3, alike, r4), (4, everyone, r5)
+        (0, everyone, r1), (1, everyone, g2), (4, alike, r4), (5, everyone, r5)
     ):
         whole(phase, team, dst).wait_send()
+    for phase, begin, count in stages:
+        skip = 1 if begin == 0 else 0
+        arrived(phase, qall, begin + skip, count - skip).wait_send()
 
 
 def solution(mesh):
@@ -285,6 +300,7 @@
             in_specs=[smem, smem, vmem, vmem, vmem] + [hbm] * len(big),
             out_specs=vmem,
             scratch_shapes=[pltpu.VMEM(shape, BF16) for shape in held_in] + [
+                pltpu.VMEM((PAIR * rows * cache.shape[2], lat), BF16),
                 pltpu.VMEM((n, held, LANES), F32),
                 pltpu.VMEM((n, held, LANES), F32),
                 pltpu.VMEM((n, held, LANES), F32),
@@ -297,8 +313,8 @@
                 pltpu.VMEM((n, rows, width), F32),
                 pltpu.SemaphoreType.DMA((17,)),
                 pltpu.SemaphoreType.DMA((2,)),
-                pltpu.SemaphoreType.DMA((5,)),
-                pltpu.SemaphoreType.DMA((5,)),
+                pltpu.SemaphoreType.DMA((6,)),
+                pltpu.SemaphoreType.DMA((6,)),
             ],
             compiler_params=pltpu.CompilerParams(
                 collective_id=0, has_side_effects=True, vmem_limit_bytes=56 * 1024 * 1024

time: 34.8 us -> 34.8 us (level)
  no operation moved by 1% of the time
where the time goes in v4:
time: 34.8 us; the launch traced here: 34.6 us
  Pallas kernels  33.3 us (96%)
  local copies, waits for them, and re-layouts  1.26 us (4%)
    pallas_call x1, Pallas kernels, per_device(): pl.pallas_call(functools.partial(kernel, n, rows, heads, lat, pad), out_s...  33.3 us
    unnamed x1, local copies, waits for them, and re-layouts  1.26 us

profile of v4, /device:TPU:0, one launch (start us, length us, event | category | flops | bytes accessed | tf_op | source)
XLA Modules:
  0.0 34.6 jit_solution(13622155447089081987)
XLA Ops:
  0.0 33.3 %shard_map.118 = bf16[2,448]{1,0:T(2,128)(2,1)} custom-call(s32[2]{0:T(128)} %lengths.1, s32[2,32]{1,0:T(2,128)} %blocks.1, bf16[2,448]{1,0:T(2,128)(2,1)} %hidden.1, f32[12,128]{1,0:T(8,128)} %bitcast.4, f32[1,512]{1,0:T(1,128)} %bitcast.5, bf16[448,1536]{1,0:T(8,128)(2,1)} %q_down.1, bf16[448,576]{1,0:T(8,128)(2,1)} %kv_down.1, bf16[1536,1536]{1,0:T(8,128)(2,1)} %q_up.1, ...), custom_call_target="tpu_custom_call" | custom-call | tf_op jit(solution)/shard_map/pallas_call | solution.py:297
  33.3 1.3 %copy.14 = bf16[2,448]{1,0:T(2,128)(2,1)} copy(bf16[2,448]{1,0:T(2,128)(2,1)} %shard_map.118) | data formatting | bytes 3584

commit v5 on v4

--- a/solution.py
+++ b/solution.py
@@ -61,12 +61,7 @@
 
     l_qd = load(q_down, v_qd)
     l_kd = load(kv_down, v_kd)
-    l_qu = load(q_up, v_qu, 4)
-    l_uk = load(w_uk, v_uk)
     core = lax.rem(me, PAIR)
-    l_ca = load(cache, v_ca.at[core])
-    l_uv = load(w_uv, v_uv)
-    l_op = load(o_proj, v_op, 8)
 
     def arrive(copies):
         for copy in copies:
@@ -132,12 +127,9 @@
     r1[me] = s1[me]
     pl.semaphore_wait(barrier, n - 1)
     send_all(0, everyone, lambda peer: s1.at[peer], r1)
-    partner = me + 1 - 2 * core
-    share = pltpu.make_async_remote_copy(
-        src_ref=cache, dst_ref=v_ca.at[core], send_sem=pair_sem.at[0], recv_sem=pair_sem.at[1],
-        device_id={"ctx": partner}, device_id_type=MESH,
-    )
-    share.start()
+    l_qu = load(q_up, v_qu, 4)
+    l_uk = load(w_uk, v_uk)
+    l_ca = load(cache, v_ca.at[core])
 
     tokens = cache.shape[2]
     token = lax.broadcasted_iota(jnp.int32, (1, PAIR * tokens), 1)
@@ -163,6 +155,14 @@
     wait_all(0, everyone, r1)
     g2[me] = jnp.sum(r1[...], axis=0)
     send_all(1, everyone, lambda peer: g2.at[me], g2)
+    partner = me + 1 - 2 * core
+    share = pltpu.make_async_remote_copy(
+        src_ref=cache, dst_ref=v_ca.at[core], send_sem=pair_sem.at[0], recv_sem=pair_sem.at[1],
+        device_id={"ctx": partner}, device_id_type=MESH,
+    )
+    share.start()
+    l_uv = load(w_uv, v_uv)
+    l_op = load(o_proj, v_op, 8)
     wait_all(1, everyone, g2)
 
     def chunk(c):

time: 34.8 us -> 34.8 us (level)
  no operation moved by 1% of the time
where the time goes in v5:
time: 34.8 us; the launch traced here: 34.6 us
  Pallas kernels  33.3 us (96%)
  local copies, waits for them, and re-layouts  1.26 us (4%)
    pallas_call x1, Pallas kernels, per_device(): pl.pallas_call(functools.partial(kernel, n, rows, heads, lat, pad), out_s...  33.3 us
    unnamed x1, local copies, waits for them, and re-layouts  1.26 us

profile of v5, /device:TPU:0, one launch (start us, length us, event | category | flops | bytes accessed | tf_op | source)
XLA Modules:
  0.0 34.6 jit_solution(5604739347749777404)
XLA Ops:
  0.0 33.3 %shard_map.118 = bf16[2,448]{1,0:T(2,128)(2,1)} custom-call(s32[2]{0:T(128)} %lengths.1, s32[2,32]{1,0:T(2,128)} %blocks.1, bf16[2,448]{1,0:T(2,128)(2,1)} %hidden.1, f32[12,128]{1,0:T(8,128)} %bitcast.4, f32[1,512]{1,0:T(1,128)} %bitcast.5, bf16[448,1536]{1,0:T(8,128)(2,1)} %q_down.1, bf16[448,576]{1,0:T(8,128)(2,1)} %kv_down.1, bf16[1536,1536]{1,0:T(8,128)(2,1)} %q_up.1, ...), custom_call_target="tpu_custom_call" | custom-call | tf_op jit(solution)/shard_map/pallas_call | solution.py:297
  33.3 1.3 %copy.14 = bf16[2,448]{1,0:T(2,128)(2,1)} copy(bf16[2,448]{1,0:T(2,128)(2,1)} %shard_map.118) | data formatting | bytes 3584

commit v6 on v4

--- a/solution.py
+++ b/solution.py
@@ -10,7 +10,7 @@
 
 NOPE = 128
 ROPE = 64
-PAIR = 2
+SHARE = 4
 BLOCK = 64
 LANES = 128
 F32 = jnp.float32
@@ -35,7 +35,7 @@
     out,
     v_qd, v_kd, v_qu, v_uk, v_ca, v_uv, v_op, v_ct,
     s1, r1, g2, qf, qs, qall, s4, r4, s5, r5,
-    load_sem, pair_sem, send_sem, recv_sem,
+    load_sem, share_sem, send_sem, recv_sem,
 ):
     me = lax.axis_index("ctx")
     ql = q_down.shape[1]
@@ -63,8 +63,8 @@
     l_kd = load(kv_down, v_kd)
     l_qu = load(q_up, v_qu, 4)
     l_uk = load(w_uk, v_uk)
-    core = lax.rem(me, PAIR)
-    l_ca = load(cache, v_ca.at[core])
+    spot = lax.rem(me, SHARE)
+    l_ca = load(cache, v_ca.at[0])
     l_uv = load(w_uv, v_uv)
     l_op = load(o_proj, v_op, 8)
 
@@ -73,7 +73,7 @@
             copy.wait()
 
     everyone = (n, me, lambda index: index)
-    alike = (n // PAIR, me // PAIR, lambda index: index * PAIR + core)
+    alike = (n // SHARE, me // SHARE, lambda index: index * SHARE + spot)
 
     def remote(phase, src, dst, device):
         return pltpu.make_async_remote_copy(
@@ -132,16 +132,23 @@
     r1[me] = s1[me]
     pl.semaphore_wait(barrier, n - 1)
     send_all(0, everyone, lambda peer: s1.at[peer], r1)
-    partner = me + 1 - 2 * core
-    share = pltpu.make_async_remote_copy(
-        src_ref=cache, dst_ref=v_ca.at[core], send_sem=pair_sem.at[0], recv_sem=pair_sem.at[1],
-        device_id={"ctx": partner}, device_id_type=MESH,
-    )
-    share.start()
+    near = me + 1 - 2 * lax.rem(me, 2)
+    far = me + 2 - 4 * (spot // 2)
+
+    def share(step, src, slot, device):
+        return pltpu.make_async_remote_copy(
+            src_ref=src, dst_ref=v_ca.at[slot], send_sem=share_sem.at[step],
+            recv_sem=share_sem.at[step + 3], device_id={"ctx": device}, device_id_type=MESH,
+        )
+
+    swaps = [share(0, cache, 2, far), share(1, cache, 1, near)]
+    for copy in swaps:
+        copy.start()
 
     tokens = cache.shape[2]
-    token = lax.broadcasted_iota(jnp.int32, (1, PAIR * tokens), 1)
-    position = (me - core) * tokens + token
+    token = lax.broadcasted_iota(jnp.int32, (1, tokens), 1)
+    owners = (me, near, far, near + far - me)
+    position = jnp.concatenate([owner * tokens + token for owner in owners], axis=1)
     block_of = position // BLOCK
     used = []
     for r in range(rows):
@@ -150,11 +157,11 @@
             hit = hit | (block_of == blocks[r, k])
         used.append(jnp.where(hit & (position < lengths[r]), 1.0, 0.0))
     used = jnp.concatenate(used, axis=1)
-    size = n // PAIR
-    mine = me // PAIR
+    size = n // SHARE
+    mine = me // SHARE
     cut = (size + 1) // 2
-    shape = (cut * pad, rows * PAIR * tokens)
-    row_of_token = lax.broadcasted_iota(jnp.int32, shape, 1) // (PAIR * tokens)
+    shape = (cut * pad, rows * SHARE * tokens)
+    row_of_token = lax.broadcasted_iota(jnp.int32, shape, 1) // (SHARE * tokens)
     row_of_query = lax.broadcasted_iota(jnp.int32, shape, 0) % rows
     valid = (row_of_token == row_of_query) & (used > 0.5)
     if pad > kr:
@@ -187,6 +194,10 @@
         device = alike[2](around(mine, k, size))
         remote(2 if k < cut else 3, qall.at[0], qall.at[k], device).start()
 
+    swaps[0].wait_recv()
+    swaps.append(share(2, v_ca.at[2], 3, near))
+    swaps[2].start()
+
     kv_lat = kv_new[:, :lat]
     kv_mean = jnp.sum(kv_lat * kv_lat, axis=1, keepdims=True) * (1.0 / lat)
     lat_new = kv_lat * lax.rsqrt(kv_mean + 1e-06) * kv_gain[...]
@@ -197,14 +208,14 @@
         key_rows = jnp.where(own_row == r, jnp.broadcast_to(key_new[r:r + 1], (pad, kvw)), key_rows)
     own = scale * jnp.sum(query.astype(F32) * key_rows, axis=1, keepdims=True)
 
+    parts = [(slot, r) for r in range(rows) for slot in range(SHARE)]
     arrive(l_ca)
-    pltpu.make_async_remote_copy(
-        src_ref=cache, dst_ref=v_ca.at[1 - core], send_sem=pair_sem.at[0], recv_sem=pair_sem.at[1],
-        device_id={"ctx": partner}, device_id_type=MESH,
-    ).wait()
-    parts = [(half, r) for r in range(rows) for half in range(PAIR)]
-    for place, (half, r) in enumerate(parts):
-        v_ct[place * tokens:(place + 1) * tokens, :] = v_ca[half, r, :lat, :].T
+    for slot in range(SHARE):
+        if slot == 1 or slot == 3:
+            swaps[1 if slot == 1 else 2].wait_recv()
+        for r in range(rows):
+            place = parts.index((slot, r))
+            v_ct[place * tokens:(place + 1) * tokens, :] = v_ca[slot, r, :lat, :].T
 
     def arrived(phase, ref, begin, count):
         view = ref.at[pl.ds(begin, count)]
@@ -215,7 +226,7 @@
         skip = 1 if begin == 0 else 0
         arrived(phase, qall, begin + skip, count - skip).wait_recv()
         q_mat = qall[begin:begin + count].reshape(count * pad, kvw)
-        score = scale * jnp.concatenate([dot(q_mat, v_ca[half, r]) for half, r in parts], axis=1)
+        score = scale * jnp.concatenate([dot(q_mat, v_ca[slot, r]) for slot, r in parts], axis=1)
         here = valid[:count * pad]
         peak = jnp.max(jnp.where(here, score, -1e30), axis=1, keepdims=True)
         expo = jnp.where(here, jnp.exp(score - peak), 0.0)
@@ -241,7 +252,7 @@
     own_weight = jnp.exp(own - top)
     denom = jnp.sum(totals * factor, axis=0) + own_weight
     mixed = own_weight * key_rows[:, :lat]
-    for d in range(n // PAIR):
+    for d in range(n // SHARE):
         mixed = mixed + factor[d] * r4[d, :, :lat].astype(F32)
     latent = (mixed / denom).astype(BF16).astype(F32)
     arrive(l_uv)
@@ -269,6 +280,8 @@
         (0, everyone, r1), (1, everyone, g2), (4, alike, r4), (5, everyone, r5)
     ):
         whole(phase, team, dst).wait_send()
+    for copy in swaps:
+        copy.wait_send()
     for phase, begin, count in stages:
         skip = 1 if begin == 0 else 0
         arrived(phase, qall, begin + skip, count - skip).wait_send()
@@ -293,26 +306,26 @@
         cache = jnp.swapaxes(cache, 1, 2)
         big = (q_down, kv_down, q_up, w_uk, cache, w_uv, o_proj)
         held_in = [a.shape for a in big]
-        held_in[4] = (PAIR,) + cache.shape
+        held_in[4] = (SHARE,) + cache.shape
         return pl.pallas_call(
             functools.partial(kernel, n, rows, heads, lat, pad),
             out_shape=jax.ShapeDtypeStruct((rows, width), BF16),
             in_specs=[smem, smem, vmem, vmem, vmem] + [hbm] * len(big),
             out_specs=vmem,
             scratch_shapes=[pltpu.VMEM(shape, BF16) for shape in held_in] + [
-                pltpu.VMEM((PAIR * rows * cache.shape[2], lat), BF16),
+                pltpu.VMEM((SHARE * rows * cache.shape[2], lat), BF16),
                 pltpu.VMEM((n, held, LANES), F32),
                 pltpu.VMEM((n, held, LANES), F32),
                 pltpu.VMEM((n, held, LANES), F32),
                 pltpu.VMEM((rows, q_up.shape[1]), F32),
                 pltpu.VMEM((pad, kvw), F32),
-                pltpu.VMEM((n // PAIR, pad, kvw), BF16),
-                pltpu.VMEM((n // PAIR, pad, lat + LANES), BF16),
-                pltpu.VMEM((n // PAIR, pad, lat + LANES), BF16),
+                pltpu.VMEM((n // SHARE, pad, kvw), BF16),
+                pltpu.VMEM((n // SHARE, pad, lat + LANES), BF16),
+                pltpu.VMEM((n // SHARE, pad, lat + LANES), BF16),
                 pltpu.VMEM((n, rows, width), F32),
                 pltpu.VMEM((n, rows, width), F32),
                 pltpu.SemaphoreType.DMA((17,)),
-                pltpu.SemaphoreType.DMA((2,)),
+                pltpu.SemaphoreType.DMA((6,)),
                 pltpu.SemaphoreType.DMA((6,)),
                 pltpu.SemaphoreType.DMA((6,)),
             ],

time: 34.8 us -> 39.3 us (1.13)
  Pallas kernels: 33.3 us -> 37.9 us
    pallas_call x1, Pallas kernels: 33.3 us -> 37.9 us  [per_device(): pl.pallas_call(functools.partial(kernel, n, rows, heads, lat, pad), out_s...]
where the time goes in v6:
time: 39.3 us; the launch traced here: 39.2 us
  Pallas kernels  37.9 us (96%)
  local copies, waits for them, and re-layouts  1.26 us (3%)
    pallas_call x1, Pallas kernels, per_device(): pl.pallas_call(functools.partial(kernel, n, rows, heads, lat, pad), out_s...  37.9 us
    unnamed x1, local copies, waits for them, and re-layouts  1.26 us

profile of v6, /device:TPU:0, one launch (start us, length us, event | category | flops | bytes accessed | tf_op | source)
XLA Modules:
  0.0 39.2 jit_solution(1442112134494665168)
XLA Ops:
  0.0 37.9 %shard_map.118 = bf16[2,448]{1,0:T(2,128)(2,1)} custom-call(s32[2]{0:T(128)} %lengths.1, s32[2,32]{1,0:T(2,128)} %blocks.1, bf16[2,448]{1,0:T(2,128)(2,1)} %hidden.1, f32[12,128]{1,0:T(8,128)} %bitcast.4, f32[1,512]{1,0:T(1,128)} %bitcast.5, bf16[448,1536]{1,0:T(8,128)(2,1)} %q_down.1, bf16[448,576]{1,0:T(8,128)(2,1)} %kv_down.1, bf16[1536,1536]{1,0:T(8,128)(2,1)} %q_up.1, ...), custom_call_target="tpu_custom_call" | custom-call | tf_op jit(solution)/shard_map/pallas_call | solution.py:310
  37.9 1.3 %copy.14 = bf16[2,448]{1,0:T(2,128)(2,1)} copy(bf16[2,448]{1,0:T(2,128)(2,1)} %shard_map.118) | data formatting | bytes 3584

commit v7 on v4

--- a/solution.py
+++ b/solution.py
@@ -252,15 +252,18 @@
     arrive(l_op)
     width = out.shape[1]
     group = math.lcm(width, 2 * LANES)
-    for g in range(n * width // group):
-        part = dot(head_out, v_op[:, g * group:(g + 1) * group])
-        for i in range(group // width):
-            d = g * (group // width) + i
-            s5[d] = part[:, i * width:(i + 1) * width]
-
-            @pl.when(me != d)
-            def _():
-                remote(5, s5.at[d], r5.at[me], d).start()
+    per = group // width
+    groups = n // per
+    home = me // per
+    seat = me - home * per
+    for off in sorted(range(groups), key=lambda off: -min(off, groups - off)):
+        g = around(home, off, groups)
+        part = dot(head_out, v_op[:, pl.ds(pl.multiple_of(g * group, 2 * LANES), group)])
+        for i in range(per):
+            s5[g * per + i] = part[:, i * width:(i + 1) * width]
+        for i in range(0 if off else 1, per):
+            d = g * per + (i if off else around(seat, i, per))
+            remote(5, s5.at[d], r5.at[me], d).start()
 
     r5[me] = s5[me]
     wait_all(5, everyone, r5)

time: 34.8 us -> 35.4 us (1.017)
  Pallas kernels: 33.3 us -> 33.9 us
    pallas_call x1, Pallas kernels: 33.3 us -> 33.9 us  [per_device(): pl.pallas_call(functools.partial(kernel, n, rows, heads, lat, pad), out_s...]
where the time goes in v7:
time: 35.4 us; the launch traced here: 35.2 us
  Pallas kernels  33.9 us (96%)
  local copies, waits for them, and re-layouts  1.26 us (4%)
    pallas_call x1, Pallas kernels, per_device(): pl.pallas_call(functools.partial(kernel, n, rows, heads, lat, pad), out_s...  33.9 us
    unnamed x1, local copies, waits for them, and re-layouts  1.26 us

profile of v7, /device:TPU:0, one launch (start us, length us, event | category | flops | bytes accessed | tf_op | source)
XLA Modules:
  0.0 35.2 jit_solution(3443347462322545893)
XLA Ops:
  0.0 33.9 %shard_map.118 = bf16[2,448]{1,0:T(2,128)(2,1)} custom-call(s32[2]{0:T(128)} %lengths.1, s32[2,32]{1,0:T(2,128)} %blocks.1, bf16[2,448]{1,0:T(2,128)(2,1)} %hidden.1, f32[12,128]{1,0:T(8,128)} %bitcast.4, f32[1,512]{1,0:T(1,128)} %bitcast.5, bf16[448,1536]{1,0:T(8,128)(2,1)} %q_down.1, bf16[448,576]{1,0:T(8,128)(2,1)} %kv_down.1, bf16[1536,1536]{1,0:T(8,128)(2,1)} %q_up.1, ...), custom_call_target="tpu_custom_call" | custom-call | tf_op jit(solution)/shard_map/pallas_call | solution.py:300
  33.9 1.3 %copy.14 = bf16[2,448]{1,0:T(2,128)(2,1)} copy(bf16[2,448]{1,0:T(2,128)(2,1)} %shard_map.118) | data formatting | bytes 3584
